TPU v7x, 32 devices: a whole 2x2x4 slice. The times are simulated.
32 devices in a mesh: gx: 4 (over x, core), gy: 4 (over z), gz: 2 (over y).
Axes of the slice: x: 2, y: 2, z: 4, core: 2. Of those that a mesh axis runs over, the one named last changes fastest.
Arguments:
- gram_factor: bfloat16 [384, 384, 384], P(('gx', 'gy', 'gz')), may hold values from -0.3125 to 0.3125
- coupling: bfloat16 [384, 384, 128], P(('gx', 'gy', 'gz')), may hold values from -0.375 to 0.375
- order_class: int32 [384], P(('gx', 'gy', 'gz')), may hold values from 0 to 2
- first_moves: int32 [96], P(('gx', 'gy', 'gz')), may hold values from 0 to 11, as said below
- second_moves: int32 [96], P(('gx', 'gy', 'gz')), may hold values from 0 to 11, as said below
- trace_index: int32 [384, 128], P(('gx', 'gy', 'gz')), may hold values from 1 to 322, as said below
- owner_index: int32 [384, 128], P(('gx', 'gy', 'gz')), may hold values from 0 to 255
- traces: bfloat16 [64, 4, 32, 256], P('gx', 'gy', 'gz'), may hold values from -6 to 6
Outputs:
- applied: float32 [64, 4, 32, 256], P('gx', 'gy', 'gz')
Inputs may be any that keep to these rules, and one draw needn't show every extreme that they name: `first_moves`: on each device the 3 entries are distinct slots. `second_moves`: on each device the 3 entries are distinct slots. `trace_index`: never a corner cell of the extended grid.
All inputs are finite; a program needn't handle non-finite values.
Results may differ from a plain program's by a relative error of at most 0.0044.
Values may be sent and summed in bfloat16 or wider, within the bound.
A program may use at most 64 MiB of HBM per device.

v0:
```python
import jax
import jax.numpy as jnp
from jax import lax
from jax.sharding import PartitionSpec as P


def swapped(block, axis, bit):
    count = lax.axis_size(axis)
    route = []
    for low in range(count):
        high = low | 1 << bit
        if high != low and high < count:
            route += [(low, high), (high, low)]
    return lax.ppermute(block, axis, route)


def with_halo(block, sides, width):
    for axis, dim in sides:
        count = lax.axis_size(axis)
        forward = [(i, i + 1) for i in range(count - 1)]
        backward = [(target, source) for source, target in forward]
        low = lax.ppermute(
            lax.slice_in_dim(block, block.shape[dim] - width, None, axis=dim), axis, forward
        )
        high = lax.ppermute(lax.slice_in_dim(block, 0, width, axis=dim), axis, backward)
        block = jnp.concatenate([low, block, high], axis=dim)
    return block


def product_of(masked, coupling):
    return jnp.einsum("ewv,evk->ewk", masked, coupling, preferred_element_type=jnp.float32).astype(
        jnp.bfloat16
    )


def body(
    gram_factor, coupling, order_class, first_moves, second_moves, trace_index, owner_index, traces
):
    width_full = gram_factor.shape[1]
    rows = lax.broadcasted_iota(jnp.int32, (1, width_full), 1)
    widths = width_full * (2 + order_class) // 4
    keep = (rows < widths[:, None]).astype(gram_factor.dtype)
    masked = gram_factor * keep[:, :, None]
    second_bit = lax.axis_size("gz").bit_length() - 1
    operator = product_of(masked, coupling)
    given = swapped(operator[first_moves], "gz", 0)
    before = swapped(operator[second_moves], ("gy", "gz"), second_bit)
    matches = second_moves[:, None] == first_moves[None, :]
    flagged = jnp.any(matches, axis=1).astype(jnp.bfloat16)
    patch = jnp.einsum(
        "ij,jwk->iwk", matches.astype(jnp.bfloat16), given, preferred_element_type=jnp.float32
    ).astype(jnp.bfloat16)
    patch_in, flag_in = swapped((patch, flagged), ("gy", "gz"), second_bit)
    given_two = jnp.where(flag_in[:, None, None] > 0.5, patch_in, before)
    operator = operator.at[first_moves].set(given)
    operator = operator.at[second_moves].set(given_two)
    rows_x = traces.shape[0]
    rows_z = traces.shape[2]
    columns = traces.shape[3]
    targets = owner_index.reshape(-1)

    def apply_field(field):
        extended = with_halo(field, (("gx", 0), ("gz", 1)), 1)
        flattened = extended.reshape(-1, columns)
        gathered = flattened[trace_index]
        tested = jnp.einsum(
            "ewk,ekr->ewr", operator, gathered, preferred_element_type=jnp.float32
        ).astype(jnp.bfloat16)
        element_out = jnp.einsum(
            "ewk,ewr->ekr", operator, tested, preferred_element_type=jnp.float32
        )
        result = (
            jnp.zeros((rows_x * rows_z, columns), jnp.float32)
            .at[targets]
            .add(element_out.reshape(-1, columns))
        )
        return result.reshape(rows_x, rows_z, columns)

    first = apply_field(traces[:, 0]).astype(jnp.bfloat16)
    second = apply_field(first)
    return second[:, None]


def solution(mesh):
    return jax.shard_map(
        body,
        mesh=mesh,
        in_specs=(
            P(("gx", "gy", "gz"), None, None),
            P(("gx", "gy", "gz"), None, None),
            P(("gx", "gy", "gz")),
            P(("gx", "gy", "gz")),
            P(("gx", "gy", "gz")),
            P(("gx", "gy", "gz"), None),
            P(("gx", "gy", "gz"), None),
            P("gx", "gy", "gz", None),
        ),
        out_specs=P("gx", "gy", "gz", None),
        check_vma=False,
    )
```

profile of v0, /device:TPU:22, one launch (start us, length us, event | category | flops | bytes accessed | tf_op | source)
XLA Modules:
  0.0 78.6 jit_solution(12484273084067406166)
XLA Ops:
  0.0 0.8 and_select_fusion
  0.8 0.1 fusion.20
  0.8 0.7 compare_select_fusion.3
  1.5 0.0 copy-start.5
  1.5 3.1 %fusion.11 = bf16[12,384,128]{2,1,0:T(8,128)(2,1)S(1)} fusion(bf16[12,384,128]{2,1,0:T(8,128)(2,1)S(1)} %copy-done, bf16[12,384,384]{2,1,0:T(8,128)(2,1)} %param.8, bf16[12,384]{1,0:T(8,128)(2,1)S(1)} %fusion.20), kind=kOutput, calls=%fused_computation.17 | convolution fusion | flops 455344128 | bytes 5907456 | tf_op jit(solution)/shard_map/ewv,evk->ewk/dot_general | solution.py:31
  4.7 0.0 copy-start.6
  4.7 0.0 copy-start.1
  4.7 0.0 copy-start.3
  4.7 0.0 copy-start.4
  4.7 0.6 gather_fusion
  5.3 0.6 collective-permute-start
  5.9 1.3 %gather_fusion.1 = bf16[3,384,128]{2,1,0:T(8,128)(2,1)} fusion(bf16[12,384,128]{2,1,0:T(8,128)(2,1)S(1)} %fusion.11, s32[1024]{0:T(1024)S(1)} %pad_clamp_fusion.1), kind=kCustom, calls=%fused_computation.1 | custom fusion | bytes 589836 | tf_op jit(solution)/shard_map/gather | solution.py:47
  7.2 1.6 %collective-permute-start.3 = (bf16[3,384,128]{2,1,0:T(8,128)(2,1)}, bf16[3,384,128]{2,1,0:T(8,128)(2,1)}, u32[]{:S(2)}, u32[]{:S(2)}) collective-permute-start(bf16[3,384,128]{2,1,0:T(8,128)(2,1)} %gather_fusion.1), channel_id=1, source_target_pairs={{0,2},{2,0},{1,3},{3,1},{4,6},{6,4},{5,7},{7,5},{8,10},{10,8},{9,1... | collective-permute-start | bytes 884744 | tf_op jit(solution)/shard_map/ppermute | solution.py:14
  8.8 0.2 compare_reduce_fusion
  9.0 0.5 collective-permute-start.1
  9.5 1.9 %collective-permute-start.5 = (bf16[1,16,256]{2,1,0:T(8,128)(2,1)S(1)}, bf16[1,16,256]{2,1,0:T(8,128)(2,1)S(1)}, u32[]{:S(2)}, u32[]{:S(2)}) collective-permute-start(bf16[1,16,256]{2,1,0:T(8,128)(2,1)S(1)} %get-tuple-element.12), channel_id=1, source_target_pairs={{8,0},{16,8},{24,16},{9,1},{17,9},{25,17},{10,2},{18,10},{26,18},{... | collective-permute-start | bytes 24584 | tf_op jit(solution)/shard_map/ppermute | solution.py:25
  11.4 2.4 %collective-permute-start.4 = (bf16[1,16,256]{2,1,0:T(8,128)(2,1)S(1)}, bf16[1,16,256]{2,1,0:T(8,128)(2,1)S(1)}, u32[]{:S(2)}, u32[]{:S(2)}) collective-permute-start(bf16[1,16,256]{2,1,0:T(8,128)(2,1)S(1)} %get-tuple-element.11), channel_id=1, source_target_pairs={{0,8},{8,16},{16,24},{1,9},{9,17},{17,25},{2,10},{10,18},{18,26},{... | collective-permute-start | bytes 24584 | tf_op jit(solution)/shard_map/ppermute | solution.py:22
  13.9 0.0 collective-permute-done.5
  13.9 2.5 %collective-permute-done.4 = bf16[1,16,256]{2,1,0:T(8,128)(2,1)S(1)} collective-permute-done((bf16[1,16,256]{2,1,0:T(8,128)(2,1)S(1)}, bf16[1,16,256]{2,1,0:T(8,128)(2,1)S(1)}, u32[]{:S(2)}, u32[]{:S(2)}) %collective-permute-start.4) | collective-permute-done | bytes 8224 | tf_op jit(solution)/shard_map/ppermute | solution.py:22
  16.4 3.4 %collective-permute-start.7 = (bf16[18,1,256]{2,1,0:T(2,128)(2,1)S(1)}, bf16[18,1,256]{2,1,0:T(2,128)(2,1)S(1)}, u32[]{:S(2)}, u32[]{:S(2)}) collective-permute-start(bf16[18,1,256]{2,1,0:T(2,128)(2,1)S(1)} %get-tuple-element.8), channel_id=1, source_target_pairs={{1,0},{3,2},{5,4},{7,6},{9,8},{11,10},{13,12},{15,14},{17,16},{19,... | collective-permute-start | bytes 27656 | tf_op jit(solution)/shard_map/ppermute | solution.py:25
  19.9 1.3 %collective-permute-start.6 = (bf16[18,1,256]{2,1,0:T(2,128)(2,1)S(1)}, bf16[18,1,256]{2,1,0:T(2,128)(2,1)S(1)}, u32[]{:S(2)}, u32[]{:S(2)}) collective-permute-start(bf16[18,1,256]{2,1,0:T(2,128)(2,1)S(1)} %get-tuple-element.7), channel_id=1, source_target_pairs={{0,1},{2,3},{4,5},{6,7},{8,9},{10,11},{12,13},{14,15},{16,17},{18,... | collective-permute-start | bytes 27656 | tf_op jit(solution)/shard_map/ppermute | solution.py:22
  21.2 0.0 collective-permute-done
  21.2 0.4 fusion.14
  21.6 0.8 copy.20
  22.4 1.6 %collective-permute-start.2 = (bf16[3,384,128]{2,1,0:T(8,128)(2,1)}, bf16[3,384,128]{2,1,0:T(8,128)(2,1)}, u32[]{:S(2)}, u32[]{:S(2)}) collective-permute-start(bf16[3,384,128]{2,1,0:T(8,128)(2,1)} %copy.20), channel_id=1, source_target_pairs={{0,2},{2,0},{1,3},{3,1},{4,6},{6,4},{5,7},{7,5},{8,10},{10,8},{9,1... | collective-permute-start | bytes 884744 | tf_op jit(solution)/shard_map/ppermute | solution.py:14
  24.0 1.5 %collective-permute-done.6 = bf16[18,1,256]{2,1,0:T(2,128)(2,1)S(1)} collective-permute-done((bf16[18,1,256]{2,1,0:T(2,128)(2,1)S(1)}, bf16[18,1,256]{2,1,0:T(2,128)(2,1)S(1)}, u32[]{:S(2)}, u32[]{:S(2)}) %collective-permute-start.6) | collective-permute-done | bytes 9248 | tf_op jit(solution)/shard_map/ppermute | solution.py:22
  25.5 0.1 pad_maximum_fusion
  25.6 0.1 reshape.76
  25.7 4.8 %gather_fusion.2 = bf16[1536,256]{1,0:T(8,128)(2,1)S(1)} fusion(bf16[324,256]{1,0:T(8,128)(2,1)S(1)} %reshape.76, s32[2048]{0:T(1024)S(1)} %pad_clamp_fusion), kind=kCustom, calls=%fused_computation.2 | custom fusion | bytes 1579008 | tf_op jit(solution)/shard_map/gather | solution.py:65
  30.5 1.6 %scatter_fusion = bf16[12,384,128]{2,1,0:T(8,128)(2,1)S(1)} fusion(bf16[12,384,128]{2,1,0:T(8,128)(2,1)S(1)} %fusion.11, s32[3]{0:T(128)S(1)} %compare_select_fusion.3, bf16[3,384,128]{2,1,0:T(8,128)(2,1)} %copy-done.2), kind=kCustom, calls=%fused_computation.4 | custom fusion | bytes 884748 | tf_op jit(solution)/shard_map/scatter | solution.py:55
  32.1 0.0 collective-permute-done.3
  32.1 1.1 %broadcast_select_fusion = bf16[3,384,128]{2,1,0:T(8,128)(2,1)S(1)} fusion(bf16[3,384,128]{2,1,0:T(8,128)(2,1)} %collective-permute-done.2, bf16[3,384,128]{2,1,0:T(8,128)(2,1)} %collective-permute-done.3, pred[3]{0:T(512)(128)(4,1)S(1)} %broadcast_compare_fusion), kind=kLoop, calls=%fused_computation.21 | loop fusion | flops 147456 | bytes 884739 | tf_op jit(solution)/shard_map/jit(_where)/select_n | solution.py:54
  33.3 0.8 scatter_fusion.1
  34.0 2.4 %fusion.4 = f32[12,128,256]{2,1,0:T(8,128)} fusion(bf16[12,384,128]{2,1,0:T(8,128)(2,1)S(1)} %scatter_fusion.1, bf16[12,128,256]{2,1,0:T(8,128)(2,1)S(1)} %bitcast.32), kind=kOutput, calls=%fused_computation.12 | convolution fusion | flops 605159424 | bytes 3538944 | tf_op jit(solution)/shard_map/ewk,ewr->ekr/dot_general | solution.py:69
  36.4 9.3 %scatter_custom_fusion.2 = f32[256,256]{1,0:T(8,128)S(1)} fusion(s32[1536]{0:T(1024)S(1)} %fusion.22, f32[1536,256]{1,0:T(8,128)} %bitcast.35, f32[]{:T(128)} %constant.12.clone.1), kind=kCustom, calls=%fused_computation.26 | custom fusion | flops 393216 | bytes 262656 | tf_op jit(solution)/shard_map/scatter-add | solution.py:75
  45.7 1.9 %collective-permute-start.9 = (bf16[1,16,256]{2,1,0:T(8,128)(2,1)S(1)}, bf16[1,16,256]{2,1,0:T(8,128)(2,1)S(1)}, u32[]{:S(2)}, u32[]{:S(2)}) collective-permute-start(bf16[1,16,256]{2,1,0:T(8,128)(2,1)S(1)} %get-tuple-element.10), channel_id=1, source_target_pairs={{8,0},{16,8},{24,16},{9,1},{17,9},{25,17},{10,2},{18,10},{26,18},{... | collective-permute-start | bytes 24584 | tf_op jit(solution)/shard_map/ppermute | solution.py:25
  47.7 2.4 %collective-permute-start.8 = (bf16[1,16,256]{2,1,0:T(8,128)(2,1)S(1)}, bf16[1,16,256]{2,1,0:T(8,128)(2,1)S(1)}, u32[]{:S(2)}, u32[]{:S(2)}) collective-permute-start(bf16[1,16,256]{2,1,0:T(8,128)(2,1)S(1)} %get-tuple-element.9), channel_id=1, source_target_pairs={{0,8},{8,16},{16,24},{1,9},{9,17},{17,25},{2,10},{10,18},{18,26},{... | collective-permute-start | bytes 24584 | tf_op jit(solution)/shard_map/ppermute | solution.py:22
  50.1 0.0 collective-permute-done.9
  50.1 2.5 %collective-permute-done.8 = bf16[1,16,256]{2,1,0:T(8,128)(2,1)S(1)} collective-permute-done((bf16[1,16,256]{2,1,0:T(8,128)(2,1)S(1)}, bf16[1,16,256]{2,1,0:T(8,128)(2,1)S(1)}, u32[]{:S(2)}, u32[]{:S(2)}) %collective-permute-start.8) | collective-permute-done | bytes 8224 | tf_op jit(solution)/shard_map/ppermute | solution.py:22
  52.7 3.0 %collective-permute-start.11 = (bf16[18,1,256]{2,1,0:T(2,128)(2,1)S(1)}, bf16[18,1,256]{2,1,0:T(2,128)(2,1)S(1)}, u32[]{:S(2)}, u32[]{:S(2)}) collective-permute-start(bf16[18,1,256]{2,1,0:T(2,128)(2,1)S(1)} %get-tuple-element.6), channel_id=1, source_target_pairs={{1,0},{3,2},{5,4},{7,6},{9,8},{11,10},{13,12},{15,14},{17,16},{19,... | collective-permute-start | bytes 27656 | tf_op jit(solution)/shard_map/ppermute | solution.py:25
  55.7 1.5 %collective-permute-start.10 = (bf16[18,1,256]{2,1,0:T(2,128)(2,1)S(1)}, bf16[18,1,256]{2,1,0:T(2,128)(2,1)S(1)}, u32[]{:S(2)}, u32[]{:S(2)}) collective-permute-start(bf16[18,1,256]{2,1,0:T(2,128)(2,1)S(1)} %get-tuple-element.5), channel_id=1, source_target_pairs={{0,1},{2,3},{4,5},{6,7},{8,9},{10,11},{12,13},{14,15},{16,17},{18,... | collective-permute-start | bytes 27656 | tf_op jit(solution)/shard_map/ppermute | solution.py:22
  57.2 0.0 collective-permute-done.11
  57.2 4.2 %collective-permute-done.10 = bf16[18,1,256]{2,1,0:T(2,128)(2,1)S(1)} collective-permute-done((bf16[18,1,256]{2,1,0:T(2,128)(2,1)S(1)}, bf16[18,1,256]{2,1,0:T(2,128)(2,1)S(1)}, u32[]{:S(2)}, u32[]{:S(2)}) %collective-permute-start.10) | collective-permute-done | bytes 9248 | tf_op jit(solution)/shard_map/ppermute | solution.py:22
  61.4 0.1 pad_maximum_fusion.1
  61.5 0.1 reshape.78
  61.6 4.8 %gather_fusion.3 = bf16[1536,256]{1,0:T(8,128)(2,1)S(1)} fusion(bf16[324,256]{1,0:T(8,128)(2,1)S(1)} %reshape.78, s32[2048]{0:T(1024)S(1)} %pad_clamp_fusion), kind=kCustom, calls=%fused_computation.3 | custom fusion | bytes 1579008 | tf_op jit(solution)/shard_map/gather | solution.py:65
  66.3 2.4 %fusion.2 = f32[12,128,256]{2,1,0:T(8,128)} fusion(bf16[12,384,128]{2,1,0:T(8,128)(2,1)S(1)} %scatter_fusion.1, bf16[12,128,256]{2,1,0:T(8,128)(2,1)S(1)} %bitcast.33), kind=kOutput, calls=%fused_computation.10 | convolution fusion | flops 605159424 | bytes 3538944 | tf_op jit(solution)/shard_map/ewk,ewr->ekr/dot_general | solution.py:69
  68.7 9.9 %scatter_custom_fusion.3 = f32[256,256]{1,0:T(8,128)} fusion(s32[1536]{0:T(1024)S(1)} %fusion.22, f32[1536,256]{1,0:T(8,128)} %bitcast.34, f32[]{:T(128)} %constant.12.clone.1), kind=kCustom, calls=%fused_computation.24 | custom fusion | flops 393216 | bytes 262656 | tf_op jit(solution)/shard_map/scatter-add | solution.py:75
  (25 shorter events, 0.2 us)
Async XLA Ops:
  0.0 1.5 %copy-start = (bf16[12,384,128]{2,1,0:T(8,128)(2,1)S(1)}, bf16[12,384,128]{2,1,0:T(8,128)(2,1)}, u32[]{:S(2)}) copy-start(bf16[12,384,128]{2,1,0:T(8,128)(2,1)} %param.9) | copy-start | bytes 3538948
  1.5 4.4 %copy-start.5 = (s32[3]{0:T(128)S(1)}, s32[3]{0:T(128)}, u32[]{:S(2)}) copy-start(s32[3]{0:T(128)} %param.12) | copy-start | bytes 40
  4.7 4.1 %copy-start.6 = (s32[3]{0:T(128)S(1)}, s32[3]{0:T(128)}, u32[]{:S(2)}) copy-start(s32[3]{0:T(128)} %param.11) | copy-start | bytes 40
  4.7 4.8 %copy-start.1 = (bf16[16,1,16,256]{3,2,1,0:T(8,128)(2,1)S(1)}, bf16[16,1,16,256]{3,2,1,0:T(8,128)(2,1)}, u32[]{:S(2)}) copy-start(bf16[16,1,16,256]{3,2,1,0:T(8,128)(2,1)} %param.15) | copy-start | bytes 393220
  4.7 9.1 %copy-start.3 = (s32[12,128]{1,0:T(8,128)S(1)}, s32[12,128]{1,0:T(8,128)}, u32[]{:S(2)}) copy-start(s32[12,128]{1,0:T(8,128)} %param.13) | copy-start | bytes 18436
  4.7 9.1 %copy-start.4 = (s32[12,128]{1,0:T(8,128)S(1)}, s32[12,128]{1,0:T(8,128)}, u32[]{:S(2)}) copy-start(s32[12,128]{1,0:T(8,128)} %param.14) | copy-start | bytes 18436
  5.3 15.8 %collective-permute-start = (bf16[3,384,128]{2,1,0:T(8,128)(2,1)S(1)}, bf16[3,384,128]{2,1,0:T(8,128)(2,1)S(1)}, u32[]{:S(2)}, u32[]{:S(2)}) collective-permute-start(bf16[3,384,128]{2,1,0:T(8,128)(2,1)S(1)} %gather_fusion), channel_id=1, source_target_pairs={{0,1},{1,0},{2,3},{3,2},{4,5},{5,4},{6,7},{7,6},{8,9},{9,8},{10,11... | collective-permute-start | bytes 884744 | tf_op jit(solution)/shard_map/ppermute | solution.py:14
  7.2 24.9 %collective-permute-start.3 = (bf16[3,384,128]{2,1,0:T(8,128)(2,1)}, bf16[3,384,128]{2,1,0:T(8,128)(2,1)}, u32[]{:S(2)}, u32[]{:S(2)}) collective-permute-start(bf16[3,384,128]{2,1,0:T(8,128)(2,1)} %gather_fusion.1), channel_id=1, source_target_pairs={{0,2},{2,0},{1,3},{3,1},{4,6},{6,4},{5,7},{7,5},{8,10},{10,8},{9,1... | collective-permute-start | bytes 884744 | tf_op jit(solution)/shard_map/ppermute | solution.py:14
  9.0 15.0 %collective-permute-start.1 = (bf16[3]{0:T(256)(128)(2,1)S(1)}, bf16[3]{0:T(256)(128)(2,1)S(1)}, u32[]{:S(2)}, u32[]{:S(2)}) collective-permute-start(bf16[3]{0:T(256)(128)(2,1)S(1)} %convert_element_type.31), channel_id=1, source_target_pairs={{0,2},{2,0},{1,3},{3,1},{4,6},{6,4},{5,7},{7,5},{8,10},{10,8},{9,1... | collective-permute-start | bytes 26 | tf_op jit(solution)/shard_map/ppermute | solution.py:14
  9.5 4.4 %collective-permute-start.5 = (bf16[1,16,256]{2,1,0:T(8,128)(2,1)S(1)}, bf16[1,16,256]{2,1,0:T(8,128)(2,1)S(1)}, u32[]{:S(2)}, u32[]{:S(2)}) collective-permute-start(bf16[1,16,256]{2,1,0:T(8,128)(2,1)S(1)} %get-tuple-element.12), channel_id=1, source_target_pairs={{8,0},{16,8},{24,16},{9,1},{17,9},{25,17},{10,2},{18,10},{26,18},{... | collective-permute-start | bytes 24584 | tf_op jit(solution)/shard_map/ppermute | solution.py:25
  11.4 5.0 %collective-permute-start.4 = (bf16[1,16,256]{2,1,0:T(8,128)(2,1)S(1)}, bf16[1,16,256]{2,1,0:T(8,128)(2,1)S(1)}, u32[]{:S(2)}, u32[]{:S(2)}) collective-permute-start(bf16[1,16,256]{2,1,0:T(8,128)(2,1)S(1)} %get-tuple-element.11), channel_id=1, source_target_pairs={{0,8},{8,16},{16,24},{1,9},{9,17},{17,25},{2,10},{10,18},{18,26},{... | collective-permute-start | bytes 24584 | tf_op jit(solution)/shard_map/ppermute | solution.py:22
  16.4 7.6 %collective-permute-start.7 = (bf16[18,1,256]{2,1,0:T(2,128)(2,1)S(1)}, bf16[18,1,256]{2,1,0:T(2,128)(2,1)S(1)}, u32[]{:S(2)}, u32[]{:S(2)}) collective-permute-start(bf16[18,1,256]{2,1,0:T(2,128)(2,1)S(1)} %get-tuple-element.8), channel_id=1, source_target_pairs={{1,0},{3,2},{5,4},{7,6},{9,8},{11,10},{13,12},{15,14},{17,16},{19,... | collective-permute-start | bytes 27656 | tf_op jit(solution)/shard_map/ppermute | solution.py:25
  19.9 5.7 %collective-permute-start.6 = (bf16[18,1,256]{2,1,0:T(2,128)(2,1)S(1)}, bf16[18,1,256]{2,1,0:T(2,128)(2,1)S(1)}, u32[]{:S(2)}, u32[]{:S(2)}) collective-permute-start(bf16[18,1,256]{2,1,0:T(2,128)(2,1)S(1)} %get-tuple-element.7), channel_id=1, source_target_pairs={{0,1},{2,3},{4,5},{6,7},{8,9},{10,11},{12,13},{14,15},{16,17},{18,... | collective-permute-start | bytes 27656 | tf_op jit(solution)/shard_map/ppermute | solution.py:22
  21.2 2.8 %copy-start.2 = (bf16[3,384,128]{2,1,0:T(8,128)(2,1)}, bf16[3,384,128]{2,1,0:T(8,128)(2,1)S(1)}, u32[]{:S(2)}) copy-start(bf16[3,384,128]{2,1,0:T(8,128)(2,1)S(1)} %collective-permute-done) | copy-start | bytes 884740
  22.4 9.7 %collective-permute-start.2 = (bf16[3,384,128]{2,1,0:T(8,128)(2,1)}, bf16[3,384,128]{2,1,0:T(8,128)(2,1)}, u32[]{:S(2)}, u32[]{:S(2)}) collective-permute-start(bf16[3,384,128]{2,1,0:T(8,128)(2,1)} %copy.20), channel_id=1, source_target_pairs={{0,2},{2,0},{1,3},{3,1},{4,6},{6,4},{5,7},{7,5},{8,10},{10,8},{9,1... | collective-permute-start | bytes 884744 | tf_op jit(solution)/shard_map/ppermute | solution.py:14
  45.7 4.3 %collective-permute-start.9 = (bf16[1,16,256]{2,1,0:T(8,128)(2,1)S(1)}, bf16[1,16,256]{2,1,0:T(8,128)(2,1)S(1)}, u32[]{:S(2)}, u32[]{:S(2)}) collective-permute-start(bf16[1,16,256]{2,1,0:T(8,128)(2,1)S(1)} %get-tuple-element.10), channel_id=1, source_target_pairs={{8,0},{16,8},{24,16},{9,1},{17,9},{25,17},{10,2},{18,10},{26,18},{... | collective-permute-start | bytes 24584 | tf_op jit(solution)/shard_map/ppermute | solution.py:25
  47.7 5.0 %collective-permute-start.8 = (bf16[1,16,256]{2,1,0:T(8,128)(2,1)S(1)}, bf16[1,16,256]{2,1,0:T(8,128)(2,1)S(1)}, u32[]{:S(2)}, u32[]{:S(2)}) collective-permute-start(bf16[1,16,256]{2,1,0:T(8,128)(2,1)S(1)} %get-tuple-element.9), channel_id=1, source_target_pairs={{0,8},{8,16},{16,24},{1,9},{9,17},{17,25},{2,10},{10,18},{18,26},{... | collective-permute-start | bytes 24584 | tf_op jit(solution)/shard_map/ppermute | solution.py:22
  52.7 4.5 %collective-permute-start.11 = (bf16[18,1,256]{2,1,0:T(2,128)(2,1)S(1)}, bf16[18,1,256]{2,1,0:T(2,128)(2,1)S(1)}, u32[]{:S(2)}, u32[]{:S(2)}) collective-permute-start(bf16[18,1,256]{2,1,0:T(2,128)(2,1)S(1)} %get-tuple-element.6), channel_id=1, source_target_pairs={{1,0},{3,2},{5,4},{7,6},{9,8},{11,10},{13,12},{15,14},{17,16},{19,... | collective-permute-start | bytes 27656 | tf_op jit(solution)/shard_map/ppermute | solution.py:25
  55.7 5.7 %collective-permute-start.10 = (bf16[18,1,256]{2,1,0:T(2,128)(2,1)S(1)}, bf16[18,1,256]{2,1,0:T(2,128)(2,1)S(1)}, u32[]{:S(2)}, u32[]{:S(2)}) collective-permute-start(bf16[18,1,256]{2,1,0:T(2,128)(2,1)S(1)} %get-tuple-element.5), channel_id=1, source_target_pairs={{0,1},{2,3},{4,5},{6,7},{8,9},{10,11},{12,13},{14,15},{16,17},{18,... | collective-permute-start | bytes 27656 | tf_op jit(solution)/shard_map/ppermute | solution.py:22
where the time goes:
time: 79 us; the launch traced here: 78.6 us
  other arithmetic  22.5 us (28%)
  starting transfers between devices  22.1 us (28%)
  local copies, waits for them, and re-layouts  14.7 us (19%)
  waiting for transfers between devices  10.7 us (14%)
  matrix products  8.28 us (10%)
    scatter-add x2, other arithmetic, apply_field(): result = jnp.zeros((rows_x * rows_z, columns), jnp.float32).at[targets].a...  19.2 us
    ppermute x4, waiting for transfers between devices, with_halo(): lax.ppermute(lax.slice_in_dim(block, block.shape[dim] - width, None, axis...  10.7 us
    ppermute x4, starting transfers between devices, with_halo(): lax.ppermute(lax.slice_in_dim(block, 0, width, axis=dim), axis, backward)  10.3 us
    gather x2, local copies, waits for them, and re-layouts, apply_field(): gathered = flattened[trace_index]  9.52 us
    ppermute x4, starting transfers between devices, with_halo(): lax.ppermute(lax.slice_in_dim(block, block.shape[dim] - width, None, axis...  7.57 us
    dot_general x2, matrix products, apply_field(): jnp.einsum('ewk,ewr->ekr', operator, tested, preferred_element_type=jnp.f...  4.7 us
    ppermute x4, starting transfers between devices, swapped(): return lax.ppermute(block, axis, route)  4.23 us
    dot_general x1, matrix products, product_of(): jnp.einsum('ewv,evk->ewk', masked, coupling, preferred_element_type=jnp.f...  3.15 us
  transfers between devices with their start and end apart: 12, of which 4 were waited for; matrix products, arithmetic and copies ran while one was open for 12% of the time, Pallas kernels for 0%

commit v1 on v0

--- a/solution.py
+++ b/solution.py
@@ -33,6 +33,20 @@
     )
 
 
+def picked(slots, operator):
+    chosen = slots[:, None] == jnp.arange(operator.shape[0])[None, :]
+    return jnp.einsum(
+        "is,swk->iwk", chosen.astype(operator.dtype), operator, preferred_element_type=jnp.float32
+    ).astype(operator.dtype)
+
+
+def placed(operator, slots, arrived):
+    numbers = jnp.arange(operator.shape[0])
+    for i in range(slots.shape[0]):
+        operator = jnp.where((numbers == slots[i])[:, None, None], arrived[i], operator)
+    return operator
+
+
 def body(
     gram_factor, coupling, order_class, first_moves, second_moves, trace_index, owner_index, traces
 ):
@@ -43,8 +57,8 @@
     masked = gram_factor * keep[:, :, None]
     second_bit = lax.axis_size("gz").bit_length() - 1
     operator = product_of(masked, coupling)
-    given = swapped(operator[first_moves], "gz", 0)
-    before = swapped(operator[second_moves], ("gy", "gz"), second_bit)
+    given = swapped(picked(first_moves, operator), "gz", 0)
+    before = swapped(picked(second_moves, operator), ("gy", "gz"), second_bit)
     matches = second_moves[:, None] == first_moves[None, :]
     flagged = jnp.any(matches, axis=1).astype(jnp.bfloat16)
     patch = jnp.einsum(
@@ -52,27 +66,31 @@
     ).astype(jnp.bfloat16)
     patch_in, flag_in = swapped((patch, flagged), ("gy", "gz"), second_bit)
     given_two = jnp.where(flag_in[:, None, None] > 0.5, patch_in, before)
-    operator = operator.at[first_moves].set(given)
-    operator = operator.at[second_moves].set(given_two)
+    operator = placed(operator, first_moves, given)
+    operator = placed(operator, second_moves, given_two)
     rows_x = traces.shape[0]
     rows_z = traces.shape[2]
     columns = traces.shape[3]
-    targets = owner_index.reshape(-1)
+    own_cells = lax.broadcasted_iota(jnp.int32, (1, rows_x * rows_z), 1)
+    into = (owner_index.reshape(-1, 1) == own_cells).astype(jnp.bfloat16)
+    cells = lax.broadcasted_iota(jnp.int32, (1, (rows_x + 2) * (rows_z + 2)), 1)
+    reads = (trace_index.reshape(-1, 1) == cells).astype(jnp.bfloat16)
+    slots, taken = trace_index.shape
+    scattered = jnp.einsum(
+        "ewk,ekn->ewn", operator, into.reshape(slots, taken, -1),
+        preferred_element_type=jnp.float32,
+    ).astype(jnp.bfloat16)
 
     def apply_field(field):
         extended = with_halo(field, (("gx", 0), ("gz", 1)), 1)
         flattened = extended.reshape(-1, columns)
-        gathered = flattened[trace_index]
+        gathered = jnp.dot(reads, flattened, preferred_element_type=jnp.float32)
+        gathered = gathered.astype(jnp.bfloat16).reshape(slots, taken, columns)
         tested = jnp.einsum(
             "ewk,ekr->ewr", operator, gathered, preferred_element_type=jnp.float32
         ).astype(jnp.bfloat16)
-        element_out = jnp.einsum(
-            "ewk,ewr->ekr", operator, tested, preferred_element_type=jnp.float32
-        )
-        result = (
-            jnp.zeros((rows_x * rows_z, columns), jnp.float32)
-            .at[targets]
-            .add(element_out.reshape(-1, columns))
+        result = jnp.einsum(
+            "ewn,ewr->nr", scattered, tested, preferred_element_type=jnp.float32
         )
         return result.reshape(rows_x, rows_z, columns)
 

time: 79 us -> 71 us (0.90)
  the two profiles are of different devices: /device:TPU:22 before, /device:TPU:0 now
where the time goes in v1:
time: 71 us; the launch traced here: 70 us
  waiting for transfers between devices  19.7 us (28%)
  starting transfers between devices  19.5 us (27%)
  matrix products  18.9 us (27%)
  other arithmetic  8.17 us (12%)
  local copies, waits for them, and re-layouts  3.39 us (5%)
    ppermute x4, waiting for transfers between devices, with_halo(): lax.ppermute(lax.slice_in_dim(block, 0, width, axis=dim), axis, backward)  9.82 us
    ppermute x4, waiting for transfers between devices, swapped(): return lax.ppermute(block, axis, route)  9.68 us
    ppermute x4, starting transfers between devices, with_halo(): lax.ppermute(lax.slice_in_dim(block, block.shape[dim] - width, None, axis...  7.53 us
    dot_general x2, matrix products, apply_field(): jnp.einsum('ewn,ewr->nr', scattered, tested, preferred_element_type=jnp.f...  7.14 us
    ppermute x4, starting transfers between devices, swapped(): return lax.ppermute(block, axis, route)  6.84 us
    ppermute x4, starting transfers between devices, with_halo(): lax.ppermute(lax.slice_in_dim(block, 0, width, axis=dim), axis, backward)  5.17 us
    eq x3, other arithmetic, placed(): numbers == slots[i]  4.81 us
    dot_general x1, matrix products, product_of(): jnp.einsum('ewv,evk->ewk', masked, coupling, preferred_element_type=jnp.f...  3.16 us
  transfers between devices with their start and end apart: 12, of which 5 were waited for; matrix products, arithmetic and copies ran while one was open for 25% of the time, Pallas kernels for 0%

profile of v1, /device:TPU:0, one launch (start us, length us, event | category | flops | bytes accessed | tf_op | source)
XLA Modules:
  0.0 70.0 jit_solution(1999828510812757450)
XLA Ops:
  0.0 1.0 %compare_reduce_fusion = pred[3]{0:T(512)(128)(4,1)S(1)} fusion(s32[3]{0:T(128)} %param.11, s32[3]{0:T(128)} %param.12), kind=kLoop, calls=%fused_computation.50 | loop fusion | flops 15 | bytes 27 | tf_op jit(solution)/shard_map/reduce_or | solution.py:63
  1.0 3.1 %collective-permute-start = (bf16[3]{0:T(256)(128)(2,1)S(1)}, bf16[3]{0:T(256)(128)(2,1)S(1)}, u32[]{:S(2)}, u32[]{:S(2)}) collective-permute-start(bf16[3]{0:T(256)(128)(2,1)S(1)} %convert_element_type.48), channel_id=1, source_target_pairs={{0,2},{2,0},{1,3},{3,1},{4,6},{6,4},{5,7},{7,5},{8,10},{10,8},{9,1... | collective-permute-start | bytes 26 | tf_op jit(solution)/shard_map/ppermute | solution.py:14
  4.0 0.7 %slice_bitcast_fusion.3 = (bf16[1,16,256]{2,1,0:T(8,128)(2,1)S(1)}, bf16[1,16,256]{2,1,0:T(8,128)(2,1)S(1)}) fusion(bf16[16,1,16,256]{3,2,1,0:T(8,128)(2,1)} %param.15), kind=kLoop, calls=%fused_computation.48 | loop fusion | bytes 32768 | tf_op jit(solution)/shard_map/slice | solution.py:23
  4.8 1.4 %collective-permute-start.4 = (bf16[1,16,256]{2,1,0:T(8,128)(2,1)S(1)}, bf16[1,16,256]{2,1,0:T(8,128)(2,1)S(1)}, u32[]{:S(2)}, u32[]{:S(2)}) collective-permute-start(bf16[1,16,256]{2,1,0:T(8,128)(2,1)S(1)} %get-tuple-element.17), channel_id=1, source_target_pairs={{0,8},{8,16},{16,24},{1,9},{9,17},{17,25},{2,10},{10,18},{18,26},{... | collective-permute-start | bytes 24584 | tf_op jit(solution)/shard_map/ppermute | solution.py:22
  6.2 1.3 %collective-permute-start.5 = (bf16[1,16,256]{2,1,0:T(8,128)(2,1)S(1)}, bf16[1,16,256]{2,1,0:T(8,128)(2,1)S(1)}, u32[]{:S(2)}, u32[]{:S(2)}) collective-permute-start(bf16[1,16,256]{2,1,0:T(8,128)(2,1)S(1)} %get-tuple-element.18), channel_id=1, source_target_pairs={{8,0},{16,8},{24,16},{9,1},{17,9},{25,17},{10,2},{18,10},{26,18},{... | collective-permute-start | bytes 24584 | tf_op jit(solution)/shard_map/ppermute | solution.py:25
  7.5 0.7 and_select_fusion
  8.2 0.1 fusion.33
  8.3 3.2 %fusion.15 = bf16[12,384,128]{2,1,0:T(8,128)(2,1)S(1)} fusion(bf16[12,384,128]{2,1,0:T(8,128)(2,1)S(1)} %copy-done, bf16[12,384,384]{2,1,0:T(8,128)(2,1)} %param.8, bf16[12,384]{1,0:T(8,128)(2,1)S(1)} %fusion.33), kind=kOutput, calls=%fused_computation.18 | convolution fusion | flops 455344128 | bytes 5907456 | tf_op jit(solution)/shard_map/ewv,evk->ewk/dot_general | solution.py:31
  11.4 0.0 copy-start.3
  11.5 1.5 %fusion.18 = bf16[3,384,128]{2,0,1:T(4,128)(2,1)} fusion(bf16[12,384,128]{2,1,0:T(8,128)(2,1)S(1)} %fusion.15, s32[3]{0:T(128)S(1)} %copy-done.2), kind=kOutput, calls=%fused_computation.19 | convolution fusion | flops 3686436 | bytes 1474572 | tf_op jit(solution)/shard_map/is,swk->iwk/dot_general | solution.py:38
  13.0 1.5 %collective-permute-start.1 = (bf16[3,384,128]{2,0,1:T(4,128)(2,1)}, bf16[3,384,128]{2,0,1:T(4,128)(2,1)S(1)}, u32[]{:S(2)}, u32[]{:S(2)}) collective-permute-start(bf16[3,384,128]{2,0,1:T(4,128)(2,1)} %fusion.18), channel_id=1, source_target_pairs={{0,1},{1,0},{2,3},{3,2},{4,5},{5,4},{6,7},{7,6},{8,9},{9,8},{10,11... | collective-permute-start | bytes 884744 | tf_op jit(solution)/shard_map/ppermute | solution.py:14
  14.5 1.6 %fusion.21 = bf16[3,384,128]{2,0,1:T(4,128)(2,1)} fusion(bf16[12,384,128]{2,1,0:T(8,128)(2,1)S(1)} %fusion.15, s32[3]{0:T(128)S(1)} %copy-done.3), kind=kOutput, calls=%fused_computation.20 | convolution fusion | flops 3686436 | bytes 1474572 | tf_op jit(solution)/shard_map/is,swk->iwk/dot_general | solution.py:38
  16.1 0.4 collective-permute-start.3
  16.5 0.6 fusion.45
  17.2 0.6 fusion.44
  17.8 1.2 %iota_compare_fusion.8 = (pred[12]{0:T(512)(128)(4,1)S(1)}, pred[12]{0:T(512)(128)(4,1)S(1)}) fusion(s32[]{:T(128)} %bitcast.8, s32[]{:T(128)} %bitcast.7), kind=kLoop, calls=%fused_computation.63 | loop fusion | flops 24 | bytes 32 | tf_op jit(solution)/shard_map/eq | solution.py:46
  19.1 1.7 %iota_compare_fusion.12 = (pred[12]{0:T(512)(128)(4,1)S(1)}, pred[12]{0:T(512)(128)(4,1)}) fusion(s32[]{:T(128)} %bitcast.4, s32[]{:T(128)} %bitcast), kind=kLoop, calls=%fused_computation.67 | loop fusion | flops 24 | bytes 32 | tf_op jit(solution)/shard_map/eq | solution.py:46
  20.8 1.9 %iota_compare_fusion.10 = (pred[12]{0:T(512)(128)(4,1)}, pred[12]{0:T(512)(128)(4,1)}) fusion(s32[]{:T(128)} %bitcast.6, s32[]{:T(128)} %bitcast.5), kind=kLoop, calls=%fused_computation.65 | loop fusion | flops 24 | bytes 32 | tf_op jit(solution)/shard_map/eq | solution.py:46
  22.7 2.3 %collective-permute-start.6 = (bf16[18,1,256]{2,1,0:T(2,128)(2,1)S(1)}, bf16[18,1,256]{2,1,0:T(2,128)(2,1)S(1)}, u32[]{:S(2)}, u32[]{:S(2)}) collective-permute-start(bf16[18,1,256]{2,1,0:T(2,128)(2,1)S(1)} %get-tuple-element.13), channel_id=1, source_target_pairs={{0,1},{2,3},{4,5},{6,7},{8,9},{10,11},{12,13},{14,15},{16,17},{18,... | collective-permute-start | bytes 27656 | tf_op jit(solution)/shard_map/ppermute | solution.py:22
  25.0 1.3 %collective-permute-start.7 = (bf16[18,1,256]{2,1,0:T(2,128)(2,1)S(1)}, bf16[18,1,256]{2,1,0:T(2,128)(2,1)S(1)}, u32[]{:S(2)}, u32[]{:S(2)}) collective-permute-start(bf16[18,1,256]{2,1,0:T(2,128)(2,1)S(1)} %get-tuple-element.14), channel_id=1, source_target_pairs={{1,0},{3,2},{5,4},{7,6},{9,8},{11,10},{13,12},{15,14},{17,16},{19,... | collective-permute-start | bytes 27656 | tf_op jit(solution)/shard_map/ppermute | solution.py:25
  26.3 0.5 broadcast_compare_fusion
  26.8 3.8 %collective-permute-done.7 = bf16[18,1,256]{2,1,0:T(2,128)(2,1)S(1)} collective-permute-done((bf16[18,1,256]{2,1,0:T(2,128)(2,1)S(1)}, bf16[18,1,256]{2,1,0:T(2,128)(2,1)S(1)}, u32[]{:S(2)}, u32[]{:S(2)}) %collective-permute-start.7) | collective-permute-done | bytes 9248 | tf_op jit(solution)/shard_map/ppermute | solution.py:25
  30.6 0.1 pad_maximum_fusion
  30.7 0.1 reshape.82
  30.8 2.2 %convolution_convert_fusion.1 = bf16[1536,256]{1,0:T(8,128)(2,1)} fusion(bf16[324,256]{1,0:T(8,128)(2,1)S(1)} %reshape.82, s32[1536]{0:T(1024)} %bitcast.64), kind=kOutput, calls=%fused_computation.3 | convolution fusion | flops 255694848 | bytes 958464 | tf_op jit(solution)/shard_map/dot_general | solution.py:87
  33.0 0.4 convolution_convert_fusion.3
  33.4 1.8 %collective-permute-start.2 = (bf16[3,384,128]{2,0,1:T(4,128)(2,1)S(1)}, bf16[3,384,128]{2,0,1:T(4,128)(2,1)S(1)}, u32[]{:S(2)}, u32[]{:S(2)}) collective-permute-start(bf16[3,384,128]{2,0,1:T(4,128)(2,1)S(1)} %convolution_convert_fusion.3), channel_id=1, source_target_pairs={{0,2},{2,0},{1,3},{3,1},{4,6},{6,4},{5,7},{7,5},{8,10},{10,8},{9,1... | collective-permute-start | bytes 884744 | tf_op jit(solution)/shard_map/ppermute | solution.py:14
  35.2 0.4 fusion.43
  35.7 9.7 %collective-permute-done.2 = bf16[3,384,128]{2,0,1:T(4,128)(2,1)S(1)} collective-permute-done((bf16[3,384,128]{2,0,1:T(4,128)(2,1)S(1)}, bf16[3,384,128]{2,0,1:T(4,128)(2,1)S(1)}, u32[]{:S(2)}, u32[]{:S(2)}) %collective-permute-start.2) | collective-permute-done | bytes 294944 | tf_op jit(solution)/shard_map/ppermute | solution.py:14
  45.4 0.3 broadcast_select_fusion
  45.7 0.4 fusion.42
  46.2 0.1 copy-done.5
  46.3 0.1 copy-done.6
  46.3 0.5 select_select_fusion
  46.9 0.1 copy-done.4
  47.0 2.3 %convolution_convert_fusion.2 = bf16[12,384,256]{2,1,0:T(8,128)(2,1)} fusion(bf16[12,384,128]{2,1,0:T(8,128)(2,1)S(1)} %select_select_fusion, s32[12,128]{1,0:T(8,128)S(1)} %copy-done.4), kind=kOutput, calls=%fused_computation.11 | convolution fusion | flops 303562752 | bytes 3545088 | tf_op jit(solution)/shard_map/ewk,ekn->ewn/dot_general | solution.py:79
  49.3 3.2 %fusion.29 = bf16[256,256]{1,0:T(8,128)(2,1)S(1)} fusion(bf16[12,384,256]{2,1,0:T(8,128)(2,1)} %convolution_convert_fusion.2, bf16[12,384,128]{2,1,0:T(8,128)(2,1)S(1)} %select_select_fusion, bf16[12,128,256]{2,1,0:T(8,128)(2,1)S(1)} %bitcast.66), kind=kOutput, calls=%fused_computation.26 | convolution fusion | flops 907214848 | bytes 4456448 | tf_op jit(solution)/shard_map/ewn,ewr->nr/dot_general | solution.py:92
  52.6 1.9 %collective-permute-start.8 = (bf16[1,16,256]{2,1,0:T(8,128)(2,1)S(1)}, bf16[1,16,256]{2,1,0:T(8,128)(2,1)S(1)}, u32[]{:S(2)}, u32[]{:S(2)}) collective-permute-start(bf16[1,16,256]{2,1,0:T(8,128)(2,1)S(1)} %get-tuple-element.15), channel_id=1, source_target_pairs={{0,8},{8,16},{16,24},{1,9},{9,17},{17,25},{2,10},{10,18},{18,26},{... | collective-permute-start | bytes 24584 | tf_op jit(solution)/shard_map/ppermute | solution.py:22
  54.5 1.3 %collective-permute-start.9 = (bf16[1,16,256]{2,1,0:T(8,128)(2,1)S(1)}, bf16[1,16,256]{2,1,0:T(8,128)(2,1)S(1)}, u32[]{:S(2)}, u32[]{:S(2)}) collective-permute-start(bf16[1,16,256]{2,1,0:T(8,128)(2,1)S(1)} %get-tuple-element.16), channel_id=1, source_target_pairs={{8,0},{16,8},{24,16},{9,1},{17,9},{25,17},{10,2},{18,10},{26,18},{... | collective-permute-start | bytes 24584 | tf_op jit(solution)/shard_map/ppermute | solution.py:25
  55.8 1.8 %collective-permute-done.9 = bf16[1,16,256]{2,1,0:T(8,128)(2,1)S(1)} collective-permute-done((bf16[1,16,256]{2,1,0:T(8,128)(2,1)S(1)}, bf16[1,16,256]{2,1,0:T(8,128)(2,1)S(1)}, u32[]{:S(2)}, u32[]{:S(2)}) %collective-permute-start.9) | collective-permute-done | bytes 8224 | tf_op jit(solution)/shard_map/ppermute | solution.py:25
  57.6 1.9 %collective-permute-start.10 = (bf16[18,1,256]{2,1,0:T(2,128)(2,1)S(1)}, bf16[18,1,256]{2,1,0:T(2,128)(2,1)S(1)}, u32[]{:S(2)}, u32[]{:S(2)}) collective-permute-start(bf16[18,1,256]{2,1,0:T(2,128)(2,1)S(1)} %get-tuple-element.11), channel_id=1, source_target_pairs={{0,1},{2,3},{4,5},{6,7},{8,9},{10,11},{12,13},{14,15},{16,17},{18,... | collective-permute-start | bytes 27656 | tf_op jit(solution)/shard_map/ppermute | solution.py:22
  59.6 1.3 %collective-permute-start.11 = (bf16[18,1,256]{2,1,0:T(2,128)(2,1)S(1)}, bf16[18,1,256]{2,1,0:T(2,128)(2,1)S(1)}, u32[]{:S(2)}, u32[]{:S(2)}) collective-permute-start(bf16[18,1,256]{2,1,0:T(2,128)(2,1)S(1)} %get-tuple-element.12), channel_id=1, source_target_pairs={{1,0},{3,2},{5,4},{7,6},{9,8},{11,10},{13,12},{15,14},{17,16},{19,... | collective-permute-start | bytes 27656 | tf_op jit(solution)/shard_map/ppermute | solution.py:25
  60.9 0.1 collective-permute-done.10
  61.0 4.2 %collective-permute-done.11 = bf16[18,1,256]{2,1,0:T(2,128)(2,1)S(1)} collective-permute-done((bf16[18,1,256]{2,1,0:T(2,128)(2,1)S(1)}, bf16[18,1,256]{2,1,0:T(2,128)(2,1)S(1)}, u32[]{:S(2)}, u32[]{:S(2)}) %collective-permute-start.11) | collective-permute-done | bytes 9248 | tf_op jit(solution)/shard_map/ppermute | solution.py:25
  65.2 0.1 pad_maximum_fusion.1
  65.3 0.1 reshape.84
  65.4 0.6 convolution_convert_fusion
  66.0 3.9 %fusion.2 = f32[256,256,1]{1,0,2:T(8,128)} fusion(bf16[12,384,256]{2,1,0:T(8,128)(2,1)} %convolution_convert_fusion.2, bf16[12,384,128]{2,1,0:T(8,128)(2,1)S(1)} %select_select_fusion, bf16[12,128,256]{2,1,0:T(8,128)(2,1)S(1)} %bitcast.67), kind=kOutput, calls=%fused_computation.4 | convolution fusion | flops 907149312 | bytes 4587520 | tf_op jit(solution)/shard_map/ewn,ewr->nr/dot_general | solution.py:92
  (32 shorter events, 0.2 us)
Async XLA Ops:
  0.0 8.3 %copy-start = (bf16[12,384,128]{2,1,0:T(8,128)(2,1)S(1)}, bf16[12,384,128]{2,1,0:T(8,128)(2,1)}, u32[]{:S(2)}) copy-start(bf16[12,384,128]{2,1,0:T(8,128)(2,1)} %param.9) | copy-start | bytes 3538948
  1.0 25.3 %collective-permute-start = (bf16[3]{0:T(256)(128)(2,1)S(1)}, bf16[3]{0:T(256)(128)(2,1)S(1)}, u32[]{:S(2)}, u32[]{:S(2)}) collective-permute-start(bf16[3]{0:T(256)(128)(2,1)S(1)} %convert_element_type.48), channel_id=1, source_target_pairs={{0,2},{2,0},{1,3},{3,1},{4,6},{6,4},{5,7},{7,5},{8,10},{10,8},{9,1... | collective-permute-start | bytes 26 | tf_op jit(solution)/shard_map/ppermute | solution.py:14
  4.8 17.9 %collective-permute-start.4 = (bf16[1,16,256]{2,1,0:T(8,128)(2,1)S(1)}, bf16[1,16,256]{2,1,0:T(8,128)(2,1)S(1)}, u32[]{:S(2)}, u32[]{:S(2)}) collective-permute-start(bf16[1,16,256]{2,1,0:T(8,128)(2,1)S(1)} %get-tuple-element.17), channel_id=1, source_target_pairs={{0,8},{8,16},{16,24},{1,9},{9,17},{17,25},{2,10},{10,18},{18,26},{... | collective-permute-start | bytes 24584 | tf_op jit(solution)/shard_map/ppermute | solution.py:22
  6.2 16.4 %collective-permute-start.5 = (bf16[1,16,256]{2,1,0:T(8,128)(2,1)S(1)}, bf16[1,16,256]{2,1,0:T(8,128)(2,1)S(1)}, u32[]{:S(2)}, u32[]{:S(2)}) collective-permute-start(bf16[1,16,256]{2,1,0:T(8,128)(2,1)S(1)} %get-tuple-element.18), channel_id=1, source_target_pairs={{8,0},{16,8},{24,16},{9,1},{17,9},{25,17},{10,2},{18,10},{26,18},{... | collective-permute-start | bytes 24584 | tf_op jit(solution)/shard_map/ppermute | solution.py:25
  8.3 3.2 %copy-start.2 = (s32[3]{0:T(128)S(1)}, s32[3]{0:T(128)}, u32[]{:S(2)}) copy-start(s32[3]{0:T(128)} %param.11) | copy-start | bytes 40
  11.4 3.1 %copy-start.3 = (s32[3]{0:T(128)S(1)}, s32[3]{0:T(128)}, u32[]{:S(2)}) copy-start(s32[3]{0:T(128)} %param.12) | copy-start | bytes 40
  13.0 9.6 %copy-start.1 = (bf16[16,1,16,256]{3,2,1,0:T(8,128)(2,1)S(1)}, bf16[16,1,16,256]{3,2,1,0:T(8,128)(2,1)}, u32[]{:S(2)}) copy-start(bf16[16,1,16,256]{3,2,1,0:T(8,128)(2,1)} %param.15) | copy-start | bytes 393220
  13.0 20.0 %collective-permute-start.1 = (bf16[3,384,128]{2,0,1:T(4,128)(2,1)}, bf16[3,384,128]{2,0,1:T(4,128)(2,1)S(1)}, u32[]{:S(2)}, u32[]{:S(2)}) collective-permute-start(bf16[3,384,128]{2,0,1:T(4,128)(2,1)} %fusion.18), channel_id=1, source_target_pairs={{0,1},{1,0},{2,3},{3,2},{4,5},{5,4},{6,7},{7,6},{8,9},{9,8},{10,11... | collective-permute-start | bytes 884744 | tf_op jit(solution)/shard_map/ppermute | solution.py:14
  16.1 19.6 %collective-permute-start.3 = (bf16[3,384,128]{2,0,1:T(4,128)(2,1)}, bf16[3,384,128]{2,0,1:T(4,128)(2,1)S(1)}, u32[]{:S(2)}, u32[]{:S(2)}) collective-permute-start(bf16[3,384,128]{2,0,1:T(4,128)(2,1)} %fusion.21), channel_id=1, source_target_pairs={{0,2},{2,0},{1,3},{3,1},{4,6},{6,4},{5,7},{7,5},{8,10},{10,8},{9,1... | collective-permute-start | bytes 884744 | tf_op jit(solution)/shard_map/ppermute | solution.py:14
  22.7 4.1 %collective-permute-start.6 = (bf16[18,1,256]{2,1,0:T(2,128)(2,1)S(1)}, bf16[18,1,256]{2,1,0:T(2,128)(2,1)S(1)}, u32[]{:S(2)}, u32[]{:S(2)}) collective-permute-start(bf16[18,1,256]{2,1,0:T(2,128)(2,1)S(1)} %get-tuple-element.13), channel_id=1, source_target_pairs={{0,1},{2,3},{4,5},{6,7},{8,9},{10,11},{12,13},{14,15},{16,17},{18,... | collective-permute-start | bytes 27656 | tf_op jit(solution)/shard_map/ppermute | solution.py:22
  25.0 5.7 %collective-permute-start.7 = (bf16[18,1,256]{2,1,0:T(2,128)(2,1)S(1)}, bf16[18,1,256]{2,1,0:T(2,128)(2,1)S(1)}, u32[]{:S(2)}, u32[]{:S(2)}) collective-permute-start(bf16[18,1,256]{2,1,0:T(2,128)(2,1)S(1)} %get-tuple-element.14), channel_id=1, source_target_pairs={{1,0},{3,2},{5,4},{7,6},{9,8},{11,10},{13,12},{15,14},{17,16},{19,... | collective-permute-start | bytes 27656 | tf_op jit(solution)/shard_map/ppermute | solution.py:25
  33.0 12.4 %copy-start.8 = (pred[3]{0:T(512)(128)(4,1)S(1)}, pred[3]{0:T(512)(128)(4,1)}, u32[]{:S(2)}) copy-start(pred[3]{0:T(512)(128)(4,1)} %broadcast_compare_fusion) | copy-start | bytes 13
  33.4 11.9 %collective-permute-start.2 = (bf16[3,384,128]{2,0,1:T(4,128)(2,1)S(1)}, bf16[3,384,128]{2,0,1:T(4,128)(2,1)S(1)}, u32[]{:S(2)}, u32[]{:S(2)}) collective-permute-start(bf16[3,384,128]{2,0,1:T(4,128)(2,1)S(1)} %convolution_convert_fusion.3), channel_id=1, source_target_pairs={{0,2},{2,0},{1,3},{3,1},{4,6},{6,4},{5,7},{7,5},{8,10},{10,8},{9,1... | collective-permute-start | bytes 884744 | tf_op jit(solution)/shard_map/ppermute | solution.py:14
  45.7 0.6 copy-start.5
  45.7 0.7 copy-start.6
  45.7 0.7 copy-start.7
  46.3 0.7 copy-start.4
  47.0 2.3 %copy-start.10 = (bf16[1536,256]{1,0:T(8,128)(2,1)S(1)}, bf16[1536,256]{1,0:T(8,128)(2,1)}, u32[]{:S(2)}) copy-start(bf16[1536,256]{1,0:T(8,128)(2,1)} %convolution_convert_fusion.1) | copy-start | bytes 2359300
  49.3 16.1 %copy-start.9 = (s32[12,128]{1,0:T(8,128)S(1)}, s32[12,128]{1,0:T(8,128)}, u32[]{:S(2)}) copy-start(s32[12,128]{1,0:T(8,128)} %param.13) | copy-start | bytes 18436
  52.6 3.2 %collective-permute-start.8 = (bf16[1,16,256]{2,1,0:T(8,128)(2,1)S(1)}, bf16[1,16,256]{2,1,0:T(8,128)(2,1)S(1)}, u32[]{:S(2)}, u32[]{:S(2)}) collective-permute-start(bf16[1,16,256]{2,1,0:T(8,128)(2,1)S(1)} %get-tuple-element.15), channel_id=1, source_target_pairs={{0,8},{8,16},{16,24},{1,9},{9,17},{17,25},{2,10},{10,18},{18,26},{... | collective-permute-start | bytes 24584 | tf_op jit(solution)/shard_map/ppermute | solution.py:22
  54.5 3.1 %collective-permute-start.9 = (bf16[1,16,256]{2,1,0:T(8,128)(2,1)S(1)}, bf16[1,16,256]{2,1,0:T(8,128)(2,1)S(1)}, u32[]{:S(2)}, u32[]{:S(2)}) collective-permute-start(bf16[1,16,256]{2,1,0:T(8,128)(2,1)S(1)} %get-tuple-element.16), channel_id=1, source_target_pairs={{8,0},{16,8},{24,16},{9,1},{17,9},{25,17},{10,2},{18,10},{26,18},{... | collective-permute-start | bytes 24584 | tf_op jit(solution)/shard_map/ppermute | solution.py:25
  57.6 3.4 %collective-permute-start.10 = (bf16[18,1,256]{2,1,0:T(2,128)(2,1)S(1)}, bf16[18,1,256]{2,1,0:T(2,128)(2,1)S(1)}, u32[]{:S(2)}, u32[]{:S(2)}) collective-permute-start(bf16[18,1,256]{2,1,0:T(2,128)(2,1)S(1)} %get-tuple-element.11), channel_id=1, source_target_pairs={{0,1},{2,3},{4,5},{6,7},{8,9},{10,11},{12,13},{14,15},{16,17},{18,... | collective-permute-start | bytes 27656 | tf_op jit(solution)/shard_map/ppermute | solution.py:22
  59.6 5.7 %collective-permute-start.11 = (bf16[18,1,256]{2,1,0:T(2,128)(2,1)S(1)}, bf16[18,1,256]{2,1,0:T(2,128)(2,1)S(1)}, u32[]{:S(2)}, u32[]{:S(2)}) collective-permute-start(bf16[18,1,256]{2,1,0:T(2,128)(2,1)S(1)} %get-tuple-element.12), channel_id=1, source_target_pairs={{1,0},{3,2},{5,4},{7,6},{9,8},{11,10},{13,12},{15,14},{17,16},{19,... | collective-permute-start | bytes 27656 | tf_op jit(solution)/shard_map/ppermute | solution.py:25

commit v2 on v0

v2 whole, which is shorter than its diff:
```python
import functools

import jax
import jax.numpy as jnp
from jax import lax
from jax.experimental import pallas as pl
from jax.experimental.pallas import tpu as pltpu
from jax.sharding import PartitionSpec as P

MESH = pl.DeviceIdType.MESH
F32 = jnp.float32
BF16 = jnp.bfloat16


def product(left, right, dims=((1,), (0,))):
    return lax.dot_general(left, right, (dims, ((), ())), preferred_element_type=F32)


def other(index):
    return index + 1 - 2 * lax.rem(index, 2)


def kernel(
    sizes,
    gram_hbm,
    coupling,
    order_class,
    first_moves,
    second_moves,
    trace_index,
    owner_index,
    traces,
    out,
    gram,
    stage_one,
    stage_two,
    recv_one,
    recv_two,
    final,
    reads_own,
    reads_halo,
    into,
    scattered,
    gathered,
    tested,
    field,
    ends_one,
    ends_two,
    halo_one,
    halo_two,
    gram_sem,
    send_one,
    arrive_one,
    send_two,
    arrive_two,
    halo_send,
    halo_arrive,
    *local,
):
    rows_x, rows_z, count_x, count_z, part = sizes
    slots, width, _ = gram.shape
    taken = coupling.shape[2]
    cells = rows_x * rows_z
    moved = stage_one.shape[1]
    parts = width // part
    ix = lax.axis_index("gx")
    iy = lax.axis_index("gy")
    iz = lax.axis_index("gz")

    loads = []
    for c in range(parts):
        span = pl.ds(c * part, part)
        load = pltpu.make_async_copy(
            gram_hbm.at[:, span, :], gram.at[:, span, :], gram_sem.at[c]
        )
        load.start()
        loads.append(load)
    halo_one[...] = jnp.zeros_like(halo_one)
    halo_two[...] = jnp.zeros_like(halo_two)

    sides = (
        (ix > 0, {"gx": ix - 1}),
        (ix < count_x - 1, {"gx": ix + 1}),
        (iz > 0, {"gz": iz - 1}),
        (iz < count_z - 1, {"gz": iz + 1}),
    )
    barrier = pltpu.get_barrier_semaphore()
    partners = ({"gz": other(iz)}, {"gy": other(iy)})
    pl.semaphore_signal(barrier, inc=1, device_id=partners[1], device_id_type=MESH)
    peers = jnp.int32(1)
    for there, device in sides:
        peers += jnp.where(there, 1, 0)

        @pl.when(there)
        def _():
            pl.semaphore_signal(barrier, inc=1, device_id=device, device_id_type=MESH)

    end_rows = lax.broadcasted_iota(jnp.int32, (2 * rows_x, cells), 0)
    end_cells = lax.broadcasted_iota(jnp.int32, (2 * rows_x, cells), 1)
    wanted = jnp.where(
        end_rows < rows_x, end_rows * rows_z, (end_rows - rows_x) * rows_z + rows_z - 1
    )
    ends_pick = jnp.where(wanted == end_cells, 1.0, 0.0).astype(BF16)

    line = lax.broadcasted_iota(jnp.int32, (part, taken), 0)

    def operator_part(c):
        loads[c].wait()
        for s in range(slots):
            limit = width * (2 + order_class[s]) // 4
            made = product(gram[s, c * part : (c + 1) * part, :], coupling[s])
            kept = jnp.where(line + c * part < limit, made, 0.0)
            local[c][s] = kept.astype(BF16)

    def round_one(c):
        return pltpu.make_async_remote_copy(
            src_ref=stage_one.at[c],
            dst_ref=recv_one.at[c],
            send_sem=send_one.at[c],
            recv_sem=arrive_one.at[c],
            device_id=partners[0],
            device_id_type=MESH,
        )

    def round_two(c):
        return pltpu.make_async_remote_copy(
            src_ref=stage_two.at[c],
            dst_ref=recv_two.at[c],
            send_sem=send_two.at[c],
            recv_sem=arrive_two.at[c],
            device_id=partners[1],
            device_id_type=MESH,
        )

    def halo_copies(number, block, ends, halo):
        sources = (
            block.at[pl.ds(0, rows_z)],
            block.at[pl.ds(cells - rows_z, rows_z)],
            ends.at[pl.ds(0, rows_x)],
            ends.at[pl.ds(rows_x, rows_x)],
        )
        copies = []
        for k, (there, device) in enumerate(sides):
            place = k + 1 - 2 * (k % 2)
            copies.append(
                pltpu.make_async_remote_copy(
                    src_ref=sources[k],
                    dst_ref=halo.at[place],
                    send_sem=halo_send.at[number, k],
                    recv_sem=halo_arrive.at[number, place],
                    device_id=device,
                    device_id_type=MESH,
                )
            )
        return copies

    def halo_start(copies):
        for (there, _), copy in zip(sides, copies):
            pl.when(there)(copy.start)

    def halo_wait(copies):
        for k, (there, _) in enumerate(sides):
            pl.when(there)(copies[k + 1 - 2 * (k % 2)].wait_recv)

    def halo_sent(copies):
        for (there, _), copy in zip(sides, copies):
            pl.when(there)(copy.wait_send)

    ends_one[...] = product(ends_pick, traces[...]).astype(BF16)
    operator_part(0)
    for i in range(moved):
        stage_one[0, i] = local[0][first_moves[i]]

    pl.semaphore_wait(barrier, peers)
    halos_one = halo_copies(0, traces, ends_one, halo_one)
    halo_start(halos_one)
    round_one(0).start()
    for c in range(1, parts):
        operator_part(c)
        for i in range(moved):
            stage_one[c, i] = local[c][first_moves[i]]
        round_one(c).start()

    wide = rows_z + 2
    number = trace_index[...]
    a = (number * (-(-65536 // wide))) >> 16
    b = number - a * wide
    cell = (a - 1) * rows_z + b - 1
    cell = jnp.where(a == 0, cells + b - 1, cell)
    cell = jnp.where(a == rows_x + 1, cells + rows_z + b - 1, cell)
    cell = jnp.where(b == 0, cells + 2 * rows_z + a - 1, cell)
    cell = jnp.where(b == rows_z + 1, cells + 2 * rows_z + rows_x + a - 1, cell)
    square = jnp.concatenate(
        [cell.astype(F32), jnp.zeros((taken - slots, taken), F32)], axis=0
    )
    upright = square.T.astype(jnp.int32)
    frame = halo_one.shape[0] * halo_one.shape[1]
    lane_own = lax.broadcasted_iota(jnp.int32, (taken, cells), 1)
    lane_halo = lax.broadcasted_iota(jnp.int32, (taken, frame), 1) + cells
    row_own = lax.broadcasted_iota(jnp.int32, (cells, taken), 0)

    def pick(s):
        column = upright[:, s : s + 1]
        reads_own[s] = jnp.where(column == lane_own, 1.0, 0.0).astype(BF16)
        reads_halo[s] = jnp.where(column == lane_halo, 1.0, 0.0).astype(BF16)

    def spread(s):
        into[s] = jnp.where(row_own == owner_index[s : s + 1, :], 1.0, 0.0).astype(BF16)

    def pass_on(c):
        round_one(c).wait_recv()
        for j in range(moved):
            value = local[c][second_moves[j]]
            for i in range(moved):
                value = jnp.where(second_moves[j] == first_moves[i], recv_one[c, i], value)
            stage_two[c, j] = value
        round_two(c).start()

    for s in range(slots):
        pick(s)
    for s in range(slots):
        gathered[s] = product(reads_own[s], traces[...]).astype(BF16)
    pass_on(0)
    for s in range(slots):
        spread(s)
    halo_wait(halos_one)

    def gather_halo(halo):
        rows = halo[...].reshape(frame, halo.shape[2])
        for s in range(slots):
            gathered[s] += product(reads_halo[s], rows).astype(BF16)

    gather_halo(halo_one)
    for c in range(1, parts):
        pass_on(c)

    total = jnp.zeros((cells, traces.shape[1]), F32)
    for c in range(parts):
        span = slice(c * part, (c + 1) * part)
        round_two(c).wait_recv()
        for s in range(slots):
            value = local[c][s]
            for i in range(moved):
                value = jnp.where(first_moves[i] == s, recv_one[c, i], value)
            for j in range(moved):
                value = jnp.where(second_moves[j] == s, recv_two[c, j], value)
            final[s, span, :] = value
        for s in range(slots):
            scattered[s, :, span] = product(
                into[s], final[s, span, :], ((1,), (1,))
            ).astype(BF16)
            tested[s, span, :] = product(final[s, span, :], gathered[s]).astype(BF16)
        for s in range(slots):
            total += product(scattered[s, :, span], tested[s, span, :])
    field[...] = total.astype(BF16)

    ends_two[...] = product(ends_pick, field[...]).astype(BF16)
    halos_two = halo_copies(1, field, ends_two, halo_two)
    halo_start(halos_two)
    for s in range(slots):
        gathered[s] = product(reads_own[s], field[...]).astype(BF16)
    halo_wait(halos_two)
    gather_halo(halo_two)
    total = jnp.zeros((cells, traces.shape[1]), F32)
    for s in range(slots):
        tested[s] = product(final[s], gathered[s]).astype(BF16)
        total += product(scattered[s], tested[s])
    out[...] = total
    for c in range(parts):
        round_one(c).wait_send()
        round_two(c).wait_send()
    halo_sent(halos_one)
    halo_sent(halos_two)


def body(
    gram_factor, coupling, order_class, first_moves, second_moves, trace_index, owner_index, traces
):
    slots, width, _ = gram_factor.shape
    taken = coupling.shape[2]
    rows_x, _, rows_z, columns = traces.shape
    cells = rows_x * rows_z
    moved = first_moves.shape[0]
    part = 128
    parts = width // part
    sizes = (rows_x, rows_z, lax.axis_size("gx"), lax.axis_size("gz"), part)
    vmem = pl.BlockSpec(memory_space=pltpu.VMEM)
    smem = pl.BlockSpec(memory_space=pltpu.SMEM)
    moving = pltpu.VMEM((parts, moved, part, taken), BF16)
    halo = pltpu.VMEM((4, rows_z, columns), BF16)
    ends = pltpu.VMEM((2 * rows_x, columns), BF16)
    result = pl.pallas_call(
        functools.partial(kernel, sizes),
        out_shape=jax.ShapeDtypeStruct((cells, columns), F32),
        in_specs=[pl.BlockSpec(memory_space=pl.ANY), vmem, smem, smem, smem, vmem, vmem, vmem],
        out_specs=vmem,
        scratch_shapes=[
            pltpu.VMEM((slots, width, width), BF16),
            moving,
            moving,
            moving,
            moving,
            pltpu.VMEM((slots, width, taken), BF16),
            pltpu.VMEM((slots, taken, cells), BF16),
            pltpu.VMEM((slots, taken, 2 * (rows_x + rows_z)), BF16),
            pltpu.VMEM((slots, cells, taken), BF16),
            pltpu.VMEM((slots, cells, width), BF16),
            pltpu.VMEM((slots, taken, columns), BF16),
            pltpu.VMEM((slots, width, columns), BF16),
            pltpu.VMEM((cells, columns), BF16),
            ends,
            ends,
            halo,
            halo,
            pltpu.SemaphoreType.DMA((parts,)),
            pltpu.SemaphoreType.DMA((parts,)),
            pltpu.SemaphoreType.DMA((parts,)),
            pltpu.SemaphoreType.DMA((parts,)),
            pltpu.SemaphoreType.DMA((parts,)),
            pltpu.SemaphoreType.DMA((2, 4)),
            pltpu.SemaphoreType.DMA((2, 4)),
        ]
        + [pltpu.VMEM((slots, part, taken), BF16)] * parts,
        compiler_params=pltpu.CompilerParams(
            collective_id=0, has_side_effects=True, vmem_limit_bytes=48 * 1024 * 1024
        ),
    )(
        gram_factor,
        coupling,
        order_class,
        first_moves,
        second_moves,
        trace_index,
        owner_index,
        traces.reshape(cells, columns),
    )
    return result.reshape(traces.shape)


def solution(mesh):
    return jax.shard_map(
        body,
        mesh=mesh,
        in_specs=(
            P(("gx", "gy", "gz"), None, None),
            P(("gx", "gy", "gz"), None, None),
            P(("gx", "gy", "gz")),
            P(("gx", "gy", "gz")),
            P(("gx", "gy", "gz")),
            P(("gx", "gy", "gz"), None),
            P(("gx", "gy", "gz"), None),
            P("gx", "gy", "gz", None),
        ),
        out_specs=P("gx", "gy", "gz", None),
        check_vma=False,
    )
```

time: 79 us -> 32 us (0.41)
  the two profiles are of different devices: /device:TPU:22 before, /device:TPU:0 now
where the time goes in v2:
time: 32 us; the launch traced here: 31.7 us
  Pallas kernels  23.4 us (73%)
  local copies, waits for them, and re-layouts  8.24 us (26%)
    pallas_call x1, Pallas kernels, body(): pl.pallas_call(functools.partial(kernel, sizes), out_shape=jax.ShapeDtype...  23.4 us
    unnamed x17, local copies, waits for them, and re-layouts  8.24 us

profile of v2, /device:TPU:0, one launch (start us, length us, event | category | flops | bytes accessed | tf_op | source)
XLA Modules:
  0.0 31.7 jit_solution(16769772806490569605)
XLA Ops:
  0.0 0.0 copy-start
  0.0 2.0 %copy-done = bf16[12,384,384]{2,1,0:T(8,128)(2,1)S(1)} copy-done((bf16[12,384,384]{2,1,0:T(8,128)(2,1)S(1)}, bf16[12,384,384]{2,1,0:T(8,128)(2,1)}, u32[]{:S(2)}) %copy-start) | copy-done | bytes 3538968
  2.0 0.0 copy-start.1
  2.0 1.3 %copy-done.1 = bf16[12,384,128]{2,1,0:T(8,128)(2,1)S(1)} copy-done((bf16[12,384,128]{2,1,0:T(8,128)(2,1)S(1)}, bf16[12,384,128]{2,1,0:T(8,128)(2,1)}, u32[]{:S(2)}) %copy-start.1) | copy-done | bytes 1179672
  3.3 0.0 copy-start.2
  3.3 0.9 %copy-done.2 = bf16[16,1,16,256]{3,2,1,0:T(8,128)(2,1)S(1)} copy-done((bf16[16,1,16,256]{3,2,1,0:T(8,128)(2,1)S(1)}, bf16[16,1,16,256]{3,2,1,0:T(8,128)(2,1)}, u32[]{:S(2)}) %copy-start.2) | copy-done | bytes 131096
  4.2 0.0 copy-start.3
  4.2 0.7 %copy-done.3 = s32[12,128]{1,0:T(8,128)S(1)} copy-done((s32[12,128]{1,0:T(8,128)S(1)}, s32[12,128]{1,0:T(8,128)}, u32[]{:S(2)}) %copy-start.3) | copy-done | bytes 6168
  4.9 0.0 copy-start.4
  4.9 0.7 %copy-done.4 = s32[12,128]{1,0:T(8,128)S(1)} copy-done((s32[12,128]{1,0:T(8,128)S(1)}, s32[12,128]{1,0:T(8,128)}, u32[]{:S(2)}) %copy-start.4) | copy-done | bytes 6168
  5.6 0.0 copy-start.5
  5.6 0.7 %copy-done.5 = s32[12]{0:T(128)S(1)} copy-done((s32[12]{0:T(128)S(1)}, s32[12]{0:T(128)}, u32[]{:S(2)}) %copy-start.5) | copy-done | bytes 72
  6.2 0.0 copy-start.6
  6.2 0.7 %copy-done.6 = s32[3]{0:T(128)S(1)} copy-done((s32[3]{0:T(128)S(1)}, s32[3]{0:T(128)}, u32[]{:S(2)}) %copy-start.6) | copy-done | bytes 36
  6.9 0.0 copy-start.7
  6.9 0.7 %copy-done.7 = s32[3]{0:T(128)S(1)} copy-done((s32[3]{0:T(128)S(1)}, s32[3]{0:T(128)}, u32[]{:S(2)}) %copy-start.7) | copy-done | bytes 36
  7.5 23.4 %shard_map.82 = f32[256,256]{1,0:T(8,128)S(1)} custom-call(bf16[12,384,384]{2,1,0:T(8,128)(2,1)S(1)} %copy-done, bf16[12,384,128]{2,1,0:T(8,128)(2,1)S(1)} %copy-done.1, s32[12]{0:T(128)S(1)} %copy-done.5, s32[3]{0:T(128)S(1)} %copy-done.6, s32[3]{0:T(128)S(1)} %copy-done.7, s32[12,128]{1,0:T(8,128)S(1)} %copy-done.3, s32[12,128]{1,0:T(8,128)S(1)} %copy-done.4, ...), custom_call_target="tpu_custom_call" | custom-call | tf_op jit(solution)/shard_map/pallas_call | solution.py:292
  31.0 0.7 %copy.11 = f32[16,1,16,256]{3,2,1,0:T(8,128)} copy(f32[16,1,16,256]{3,2,1,0:T(8,128)S(1)} %bitcast.4) | data formatting | bytes 524288
Async XLA Ops:
  0.0 2.0 %copy-start = (bf16[12,384,384]{2,1,0:T(8,128)(2,1)S(1)}, bf16[12,384,384]{2,1,0:T(8,128)(2,1)}, u32[]{:S(2)}) copy-start(bf16[12,384,384]{2,1,0:T(8,128)(2,1)} %gram_hbm.1) | copy-start | bytes 10616836
  2.0 1.3 %copy-start.1 = (bf16[12,384,128]{2,1,0:T(8,128)(2,1)S(1)}, bf16[12,384,128]{2,1,0:T(8,128)(2,1)}, u32[]{:S(2)}) copy-start(bf16[12,384,128]{2,1,0:T(8,128)(2,1)} %coupling.1) | copy-start | bytes 3538948
  3.3 0.9 %copy-start.2 = (bf16[16,1,16,256]{3,2,1,0:T(8,128)(2,1)S(1)}, bf16[16,1,16,256]{3,2,1,0:T(8,128)(2,1)}, u32[]{:S(2)}) copy-start(bf16[16,1,16,256]{3,2,1,0:T(8,128)(2,1)} %param.15) | copy-start | bytes 393220
  4.2 0.7 %copy-start.3 = (s32[12,128]{1,0:T(8,128)S(1)}, s32[12,128]{1,0:T(8,128)}, u32[]{:S(2)}) copy-start(s32[12,128]{1,0:T(8,128)} %trace_index.1) | copy-start | bytes 18436
  4.9 0.7 %copy-start.4 = (s32[12,128]{1,0:T(8,128)S(1)}, s32[12,128]{1,0:T(8,128)}, u32[]{:S(2)}) copy-start(s32[12,128]{1,0:T(8,128)} %owner_index.1) | copy-start | bytes 18436
  5.6 0.7 %copy-start.5 = (s32[12]{0:T(128)S(1)}, s32[12]{0:T(128)}, u32[]{:S(2)}) copy-start(s32[12]{0:T(128)} %order_class.1) | copy-start | bytes 148
  6.2 0.7 %copy-start.6 = (s32[3]{0:T(128)S(1)}, s32[3]{0:T(128)}, u32[]{:S(2)}) copy-start(s32[3]{0:T(128)} %first_moves.1) | copy-start | bytes 40
  6.9 0.7 %copy-start.7 = (s32[3]{0:T(128)S(1)}, s32[3]{0:T(128)}, u32[]{:S(2)}) copy-start(s32[3]{0:T(128)} %second_moves.1) | copy-start | bytes 40

commit v3 on v2

--- a/solution.py
+++ b/solution.py
@@ -23,6 +23,15 @@
 def kernel(
     sizes,
     gram_hbm,
+    coupling_hbm,
+    order_class_hbm,
+    first_moves_hbm,
+    second_moves_hbm,
+    trace_index_hbm,
+    owner_index_hbm,
+    traces_hbm,
+    out,
+    gram,
     coupling,
     order_class,
     first_moves,
@@ -30,8 +39,7 @@
     trace_index,
     owner_index,
     traces,
-    out,
-    gram,
+    input_sem,
     stage_one,
     stage_two,
     recv_one,
@@ -57,7 +65,7 @@
     halo_arrive,
     *local,
 ):
-    rows_x, rows_z, count_x, count_z, part = sizes
+    rows_x, rows_z, count_x, count_z, part, group = sizes
     slots, width, _ = gram.shape
     taken = coupling.shape[2]
     cells = rows_x * rows_z
@@ -67,6 +75,21 @@
     iy = lax.axis_index("gy")
     iz = lax.axis_index("gz")
 
+    inputs = []
+    for n, (source, held) in enumerate(
+        (
+            (coupling_hbm, coupling),
+            (order_class_hbm, order_class),
+            (first_moves_hbm, first_moves),
+            (second_moves_hbm, second_moves),
+            (traces_hbm, traces),
+            (trace_index_hbm, trace_index),
+            (owner_index_hbm, owner_index),
+        )
+    ):
+        load = pltpu.make_async_copy(source, held, input_sem.at[n])
+        load.start()
+        inputs.append(load)
     loads = []
     for c in range(parts):
         span = pl.ds(c * part, part)
@@ -166,6 +189,8 @@
         for (there, _), copy in zip(sides, copies):
             pl.when(there)(copy.wait_send)
 
+    for load in inputs:
+        load.wait()
     ends_one[...] = product(ends_pick, traces[...]).astype(BF16)
     operator_part(0)
     for i in range(moved):
@@ -235,16 +260,17 @@
         pass_on(c)
 
     total = jnp.zeros((cells, traces.shape[1]), F32)
-    for c in range(parts):
-        span = slice(c * part, (c + 1) * part)
-        round_two(c).wait_recv()
-        for s in range(slots):
-            value = local[c][s]
-            for i in range(moved):
-                value = jnp.where(first_moves[i] == s, recv_one[c, i], value)
-            for j in range(moved):
-                value = jnp.where(second_moves[j] == s, recv_two[c, j], value)
-            final[s, span, :] = value
+    for first in range(0, parts, group):
+        for c in range(first, first + group):
+            round_two(c).wait_recv()
+            for s in range(slots):
+                value = local[c][s]
+                for i in range(moved):
+                    value = jnp.where(first_moves[i] == s, recv_one[c, i], value)
+                for j in range(moved):
+                    value = jnp.where(second_moves[j] == s, recv_two[c, j], value)
+                final[s, c * part : (c + 1) * part, :] = value
+        span = slice(first * part, (first + group) * part)
         for s in range(slots):
             scattered[s, :, span] = product(
                 into[s], final[s, span, :], ((1,), (1,))
@@ -281,21 +307,28 @@
     rows_x, _, rows_z, columns = traces.shape
     cells = rows_x * rows_z
     moved = first_moves.shape[0]
-    part = 128
+    part = 64
     parts = width // part
-    sizes = (rows_x, rows_z, lax.axis_size("gx"), lax.axis_size("gz"), part)
+    sizes = (rows_x, rows_z, lax.axis_size("gx"), lax.axis_size("gz"), part, 2)
     vmem = pl.BlockSpec(memory_space=pltpu.VMEM)
-    smem = pl.BlockSpec(memory_space=pltpu.SMEM)
     moving = pltpu.VMEM((parts, moved, part, taken), BF16)
     halo = pltpu.VMEM((4, rows_z, columns), BF16)
     ends = pltpu.VMEM((2 * rows_x, columns), BF16)
     result = pl.pallas_call(
         functools.partial(kernel, sizes),
         out_shape=jax.ShapeDtypeStruct((cells, columns), F32),
-        in_specs=[pl.BlockSpec(memory_space=pl.ANY), vmem, smem, smem, smem, vmem, vmem, vmem],
+        in_specs=[pl.BlockSpec(memory_space=pltpu.HBM)] * 8,
         out_specs=vmem,
         scratch_shapes=[
             pltpu.VMEM((slots, width, width), BF16),
+            pltpu.VMEM(coupling.shape, BF16),
+            pltpu.SMEM(order_class.shape, jnp.int32),
+            pltpu.SMEM(first_moves.shape, jnp.int32),
+            pltpu.SMEM(second_moves.shape, jnp.int32),
+            pltpu.VMEM(trace_index.shape, jnp.int32),
+            pltpu.VMEM(owner_index.shape, jnp.int32),
+            pltpu.VMEM((cells, columns), BF16),
+            pltpu.SemaphoreType.DMA((7,)),
             moving,
             moving,
             moving,
@@ -322,7 +355,7 @@
         ]
         + [pltpu.VMEM((slots, part, taken), BF16)] * parts,
         compiler_params=pltpu.CompilerParams(
-            collective_id=0, has_side_effects=True, vmem_limit_bytes=48 * 1024 * 1024
+            collective_id=0, has_side_effects=True, vmem_limit_bytes=61 * 1024 * 1024
         ),
     )(
         gram_factor,

time: 32 us -> 25.7 us (0.80)
  local copies, waits for them, and re-layouts: 8.24 us -> 1.67 us
  Pallas kernels: 23.4 us -> 23.8 us
    unnamed x17 -> x1, local copies, waits for them, and re-layouts: 8.24 us -> 1.67 us
    pallas_call x1, Pallas kernels: 23.4 us -> 23.8 us  [body(): pl.pallas_call(functools.partial(kernel, sizes), out_shape=jax.ShapeDtype...]
where the time goes in v3:
time: 25.7 us; the launch traced here: 25.4 us
  Pallas kernels  23.8 us (93%)
  local copies, waits for them, and re-layouts  1.67 us (6%)
    pallas_call x1, Pallas kernels, body(): pl.pallas_call(functools.partial(kernel, sizes), out_shape=jax.ShapeDtype...  23.8 us
    unnamed x1, local copies, waits for them, and re-layouts  1.67 us

profile of v3, /device:TPU:0, one launch (start us, length us, event | category | flops | bytes accessed | tf_op | source)
XLA Modules:
  0.0 25.4 jit_solution(9078467077143636577)
XLA Ops:
  0.0 23.8 %shard_map.82 = f32[256,256]{1,0:T(8,128)} custom-call(bf16[12,384,384]{2,1,0:T(8,128)(2,1)} %gram_hbm.1, bf16[12,384,128]{2,1,0:T(8,128)(2,1)} %coupling_hbm.1, s32[12]{0:T(128)} %order_class_hbm.1, s32[3]{0:T(128)} %first_moves_hbm.1, s32[3]{0:T(128)} %second_moves_hbm.1, s32[12,128]{1,0:T(8,128)} %trace_index_hbm.1, s32[12,128]{1,0:T(8,128)} %owner_index_hbm.1, ...), custom_call_target="tpu_custom_call" | custom-call | tf_op jit(solution)/shard_map/pallas_call | solution.py:317
  23.8 1.7 %copy.11 = f32[16,1,16,256]{3,2,1,0:T(8,128)} copy(f32[16,1,16,256]{3,2,1,0:T(8,128)} %bitcast.4) | data formatting | bytes 524288
